TPU v7x, 256 devices: a whole 4x4x8 slice. The times are simulated.
256 devices in a mesh: dp: 16 (over x, y_hi, core), expert: 16 (over y_lo, z).
Axes of the slice: x: 4, y: 4 (y_hi: 2, y_lo: 2; y = y_hi * 2 + y_lo), z: 8, core: 2. Of those that a mesh axis runs over, the one named last changes fastest.
Arguments:
- tokens: bfloat16 [32768, 1024], P(('dp', 'expert')), may hold values from -6 to 6
- expert_ids: int32 [32768, 8], P(('dp', 'expert')), may hold values from 0 to 63, all different within a row; in each aligned block of 128 rows (0 to 127, 128 to 255, ...) at most 24 rows name the same one
- upstream: bfloat16 [32768, 1024], P(('dp', 'expert')), may hold values from -6 to 6
- router_weight: bfloat16 [1024, 64], replicated, may hold values from -0.1875 to 0.1875
- gate_matrix: bfloat16 [64, 384, 1024], P('expert'), may hold values from -0.1875 to 0.1875
- up_matrix: bfloat16 [64, 384, 1024], P('expert'), may hold values from -0.1875 to 0.1875
- down_matrix: bfloat16 [64, 384, 1024], P('expert'), may hold values from -0.3125 to 0.3125
Outputs:
- mixture: bfloat16 [32768, 1024], P(('dp', 'expert'))
- input_grad: bfloat16 [32768, 1024], P(('dp', 'expert'))
- router_grad: float32 [1024, 64], replicated
- gate_grad: float32 [64, 384, 1024], P('expert', 'dp')
- up_grad: float32 [64, 384, 1024], P('expert', 'dp')
- down_grad: float32 [64, 384, 1024], P('expert', 'dp')
Inputs may be any that keep to these rules, and one draw needn't show every extreme that they name: `expert_ids`: each row names 8 different experts. Among the rows of one device no expert is named more than 24 times, a bound that some block reaches.
All inputs are finite; a program needn't handle non-finite values.
Results may differ from a plain program's by a relative error of at most 0.0063.
Values may be sent and summed in bfloat16 or wider, within the bound.
No kernel may reach another device: no remote copies, remote signals or barrier semaphores. Data moves between devices by JAX's collectives and lax.ppermute only.
A program may use at most 320 MiB of HBM per device.

v0:
```python
import jax
import jax.numpy as jnp
from jax import lax
from jax.sharding import PartitionSpec as P


def slot_positions(expert_ids, experts, capacity):
    flat_ids = expert_ids.reshape(-1)
    columns = lax.broadcasted_iota(jnp.int32, (1, experts), 1)
    onehot = (flat_ids[:, None] == columns).astype(jnp.int32)
    ranking = jnp.cumsum(onehot, axis=0) - 1
    slot_numbers = jnp.sum(ranking * onehot, axis=1)
    return flat_ids * capacity + slot_numbers


def slot_sources(positions, total_slots):
    assign_count = positions.shape[0]
    return (
        jnp.full((total_slots,), -1, jnp.int32)
        .at[positions]
        .set(jnp.arange(assign_count, dtype=jnp.int32))
    )


def fill_slots(source_rows, sources, divisor):
    occupied = sources >= 0
    picked = jnp.take(source_rows, jnp.maximum(sources, 0) // divisor, axis=0)
    return jnp.where(occupied[:, None], picked, jnp.zeros_like(picked))


def backward_local(pre_gate, pre_up, logistic, act_grad):
    gate_back = (act_grad * pre_up * logistic * (1.0 + pre_gate * (1.0 - logistic))).astype(
        jnp.bfloat16
    )
    up_back = (act_grad * (pre_gate * logistic)).astype(jnp.bfloat16)
    return (gate_back, up_back)


def body(tokens, expert_ids, upstream, router_weight, gate_matrix, up_matrix, down_matrix):
    tok_rows, model_width = tokens.shape
    per_token = expert_ids.shape[1]
    exp_dev, hidden = (gate_matrix.shape[0], gate_matrix.shape[1])
    expert_peers = lax.axis_size("expert")
    experts = expert_peers * exp_dev
    capacity = tok_rows * per_token * 3 // (2 * experts)
    positions = slot_positions(expert_ids, experts, capacity)
    sources = slot_sources(positions, experts * capacity)
    send_rows = fill_slots(tokens, sources, per_token).reshape(
        expert_peers, exp_dev * capacity, model_width
    )
    recv_rows = lax.all_to_all(send_rows, "expert", split_axis=0, concat_axis=0, tiled=True)
    expert_rows = recv_rows.reshape(expert_peers, exp_dev, capacity, model_width)
    pre_gate = jnp.einsum(
        "secd,efd->secf", expert_rows, gate_matrix, preferred_element_type=jnp.float32
    )
    pre_up = jnp.einsum(
        "secd,efd->secf", expert_rows, up_matrix, preferred_element_type=jnp.float32
    )
    logistic = jax.nn.sigmoid(pre_gate)
    activated = (pre_gate * logistic * pre_up).astype(jnp.bfloat16)
    produced = jnp.einsum(
        "secf,efd->secd", activated, down_matrix, preferred_element_type=jnp.float32
    ).astype(jnp.bfloat16)
    returned = lax.all_to_all(
        produced.reshape(expert_peers, exp_dev * capacity, model_width),
        "expert",
        split_axis=0,
        concat_axis=0,
        tiled=True,
    )
    assign_out = jnp.take(returned.reshape(experts * capacity, model_width), positions, axis=0)
    assign_out = assign_out.reshape(tok_rows, per_token, model_width).astype(jnp.float32)
    logits = jnp.dot(tokens, router_weight, preferred_element_type=jnp.float32)
    chosen = jnp.take_along_axis(logits, expert_ids, axis=1)
    raised = jnp.exp(chosen)
    gate_probs = raised / jnp.sum(raised, axis=1, keepdims=True)
    mixture = jnp.sum(gate_probs[:, :, None] * assign_out, axis=1).astype(jnp.bfloat16)
    cotangent = upstream.astype(jnp.float32)
    prob_grad = jnp.sum(cotangent[:, None, :] * assign_out, axis=2)
    centered = prob_grad - jnp.sum(gate_probs * prob_grad, axis=1, keepdims=True)
    chosen_grad = gate_probs * centered
    expert_cols = lax.broadcasted_iota(jnp.int32, (1, 1, experts), 2)
    logit_grad = jnp.sum(
        jnp.where(expert_ids[:, :, None] == expert_cols, chosen_grad[:, :, None], 0.0), axis=1
    )
    router_part = jnp.dot(tokens.astype(jnp.float32).T, logit_grad, precision=lax.Precision.HIGHEST)
    router_grad = lax.psum(router_part, ("dp", "expert"))
    router_input = jnp.dot(
        logit_grad, router_weight.astype(jnp.float32).T, precision=lax.Precision.HIGHEST
    )
    out_grad = (gate_probs[:, :, None] * cotangent[:, None, :]).astype(jnp.bfloat16)
    out_grad = out_grad.reshape(tok_rows * per_token, model_width)
    send_grad = fill_slots(out_grad, sources, 1).reshape(
        expert_peers, exp_dev * capacity, model_width
    )
    recv_grad = lax.all_to_all(send_grad, "expert", split_axis=0, concat_axis=0, tiled=True)
    grad_rows = recv_grad.reshape(expert_peers, exp_dev, capacity, model_width)
    act_grad = jnp.einsum(
        "secd,efd->secf", grad_rows, down_matrix, preferred_element_type=jnp.float32
    )
    gate_back, up_back = backward_local(pre_gate, pre_up, logistic, act_grad)
    row_grad = (
        jnp.einsum("secf,efd->secd", gate_back, gate_matrix, preferred_element_type=jnp.float32)
        + jnp.einsum("secf,efd->secd", up_back, up_matrix, preferred_element_type=jnp.float32)
    ).astype(jnp.bfloat16)
    returned_grads = lax.all_to_all(
        row_grad.reshape(expert_peers, exp_dev * capacity, model_width),
        "expert",
        split_axis=0,
        concat_axis=0,
        tiled=True,
    )
    per_assign = jnp.take(
        returned_grads.reshape(experts * capacity, model_width), positions, axis=0
    )
    per_assign = per_assign.reshape(tok_rows, per_token, model_width).astype(jnp.float32)
    input_grad = (jnp.sum(per_assign, axis=1) + router_input).astype(jnp.bfloat16)
    full_gate = jnp.einsum(
        "secf,secd->efd", gate_back, expert_rows, preferred_element_type=jnp.float32
    )
    full_up = jnp.einsum("secf,secd->efd", up_back, expert_rows, preferred_element_type=jnp.float32)
    full_down = jnp.einsum(
        "secf,secd->efd", activated, grad_rows, preferred_element_type=jnp.float32
    )
    gate_grad = lax.psum_scatter(full_gate, "dp", scatter_dimension=1, tiled=True)
    up_grad = lax.psum_scatter(full_up, "dp", scatter_dimension=1, tiled=True)
    down_grad = lax.psum_scatter(full_down, "dp", scatter_dimension=1, tiled=True)
    return (mixture, input_grad, router_grad, gate_grad, up_grad, down_grad)


def solution(mesh):
    in_specs = (
        P(("dp", "expert"), None),
        P(("dp", "expert"), None),
        P(("dp", "expert"), None),
        P(),
        P("expert", None, None),
        P("expert", None, None),
        P("expert", None, None),
    )
    out_specs = (
        P(("dp", "expert"), None),
        P(("dp", "expert"), None),
        P(),
        P("expert", "dp", None),
        P("expert", "dp", None),
        P("expert", "dp", None),
    )
    return jax.shard_map(body, mesh=mesh, in_specs=in_specs, out_specs=out_specs, check_vma=False)
```

profile of v0, /device:TPU:2, one launch (start us, length us, event | category | flops | bytes accessed | tf_op | source)
XLA Modules:
  0.0 670.4 jit_solution(13618022292784977458)
XLA Ops:
  10.9 34.2 %reduce-window.6 = s32[64,8,128]{2,1,0:T(8,128)} reduce-window(s32[64,8,128]{2,1,0:T(8,128)} %fusion.43, s32[]{:T(128)} %constant.85.clone.1), window={size=1x1x128 pad=0_0x0_0x127_0}, to_apply=%region_1.2 | reduce-window | flops 8323072 | bytes 524292 | tf_op jit(solution)/shard_map/reduce-window
  49.3 4.3 scatter_custom_fusion
  53.8 5.8 gather_fusion
  61.9 81.5 %all_to_all.20 = bf16[16,96,1024]{2,1,0:T(8,128)(2,1)S(1)} all-to-all(bf16[16,96,1024]{2,1,0:T(8,128)(2,1)S(1)} %select_select_fusion.1), channel_id=1, replica_groups=mesh['dp'=16,'expert'=16] {'expert'}, dimensions={0} | all-to-all | bytes 6291456 | tf_op jit(solution)/shard_map/all_to_all | solution.py:51
  146.4 3.5 fusion.27
  153.9 4.8 all-to-all-start.1
  160.0 7.0 %gather_fusion.2 = f32[1024]{0:T(1024)S(1)} fusion(f32[128,64]{0,1:T(8,128)S(1)} %fusion.48, s32[1024]{0:T(1024)S(1)} %reshape.214), kind=kCustom, calls=%fused_computation.4 | custom fusion | bytes 16384 | tf_op jit(solution)/shard_map/jit(take_along_axis)/gather | solution.py:74
  169.2 61.6 %all-to-all-done.1 = bf16[16,96,1024]{2,1,0:T(8,128)(2,1)} async-done(((bf16[16,96,1024]{2,1,0:T(8,128)(2,1)}), bf16[16,96,1024]{2,1,0:T(8,128)(2,1)}, u32[]{:S(2)}, u32[]{:S(2)}) %all-to-all-start.1) | async-done | bytes 3145760 | tf_op jit(solution)/shard_map/all_to_all | solution.py:64
  230.8 8.3 %gather_fusion.3 = bf16[1024,1024]{1,0:T(8,128)(2,1)} fusion(bf16[1536,1024]{1,0:T(8,128)(2,1)} %bitcast.17, s32[1024]{0:T(1024)S(1)} %broadcast_clamp_fusion), kind=kCustom, calls=%fused_computation.clone | custom fusion | bytes 4198400 | tf_op jit(solution)/shard_map/jit(_take)/gather | solution.py:71
  242.1 2.7 fusion.2
  244.8 9.6 %gather_fusion.1 = bf16[1536,1024]{1,0:T(8,128)(2,1)} fusion(bf16[1024,1024]{1,0:T(8,128)(2,1)} %fusion.2, s32[2048]{0:T(1024)S(1)} %pad_clamp_fusion), kind=kCustom, calls=%fused_computation.3 | custom fusion | bytes 6297600 | tf_op jit(solution)/shard_map/jit(_take)/gather | solution.py:27
  254.4 3.4 select_select_fusion
  257.8 7.5 %all-to-all-start.2 = ((bf16[16,96,1024]{2,1,0:T(8,128)(2,1)}), bf16[16,96,1024]{2,1,0:T(8,128)(2,1)}, u32[]{:S(2)}, u32[]{:S(2)}) async-start(bf16[16,96,1024]{2,1,0:T(8,128)(2,1)} %select_select_fusion), calls=%async_computation.2 | async-start | bytes 6291456 | tf_op jit(solution)/shard_map/all_to_all | solution.py:96
  266.4 69.4 %all-to-all-done.2 = bf16[16,96,1024]{2,1,0:T(8,128)(2,1)} async-done(((bf16[16,96,1024]{2,1,0:T(8,128)(2,1)}), bf16[16,96,1024]{2,1,0:T(8,128)(2,1)}, u32[]{:S(2)}, u32[]{:S(2)}) %all-to-all-start.2) | async-done | bytes 3145760 | tf_op jit(solution)/shard_map/all_to_all | solution.py:96
  335.8 6.8 %fusion.20 = f32[4,384,1024]{2,1,0:T(8,128)} fusion(bf16[16,4,24,384]{3,2,0,1:T(8,128)(2,1)} %copy-done.7, bf16[16,4,24,1024]{3,2,1,0:T(8,128)(2,1)} %bitcast.21), kind=kOutput, calls=%fused_computation.34 | convolution fusion | flops 1207959552 | bytes 10616832 | tf_op jit(solution)/shard_map/secf,secd->efd/dot_general | solution.py:122
  342.7 6.8 %fusion.25 = (bf16[16,4,24,384]{3,2,0,1:T(8,128)(2,1)S(1)}, bf16[16,4,24,384]{3,2,0,1:T(8,128)(2,1)}) fusion(f32[4,16,24,384]{3,2,1,0:T(8,128)} %get-tuple-element.18, f32[4,16,24,384]{3,2,1,0:T(8,128)} %copy-done.12, bf16[4,384,1024]{2,1,0:T(8,128)(2,1)S(1)} %copy-done, bf16[16,4,24,1024]{3,2,1,0:T(8,128)(2,1)} %bitcast.21), kind=kOutput, calls=%fused_computation.41 | convolution fusion | flops 1215627264 | bytes 13369344 | tf_op jit(solution)/shard_map/secd,efd->secf/dot_general | solution.py:98
  350.6 4.5 convolution_bitcast_fusion.1
  355.4 6.8 %convolution_bitcast_fusion = f32[4,384,1024]{2,1,0:T(8,128)} fusion(bf16[16,4,24,384]{3,2,0,1:T(8,128)(2,1)} %get-tuple-element.14, bf16[16,4,24,1024]{3,2,1,0:T(8,128)(2,1)} %bitcast.146), kind=kOutput, calls=%fused_computation.35 | convolution fusion | flops 1207959552 | bytes 10616832 | tf_op jit(solution)/shard_map/secf,secd->efd/dot_general | solution.py:121
  362.2 4.5 fusion.5
  368.9 81.1 %all_to_all.21 = bf16[16,96,1024]{2,1,0:T(8,128)(2,1)} all-to-all(bf16[16,96,1024]{2,1,0:T(8,128)(2,1)S(1)} %bitcast.141), channel_id=1, replica_groups=mesh['dp'=16,'expert'=16] {'expert'}, dimensions={0} | all-to-all | bytes 6291456 | tf_op jit(solution)/shard_map/all_to_all | solution.py:106
  450.0 8.4 %gather_fusion.4 = bf16[1024,1024]{1,0:T(8,128)(2,1)} fusion(bf16[1536,1024]{1,0:T(8,128)(2,1)} %bitcast.139, s32[1024]{0:T(1024)S(1)} %broadcast_clamp_fusion), kind=kCustom, calls=%fused_computation.1.clone | custom fusion | bytes 4198400 | tf_op jit(solution)/shard_map/jit(_take)/gather | solution.py:113
  458.3 5.2 convert_reduce_fusion
  464.7 101.7 %all-reduce.2.cloned.1.call-done = f32[1024,64]{0,1:T(8,128)} async-done(((f32[1024,64]{0,1:T(8,128)}), f32[1024,64]{0,1:T(8,128)}) %all-reduce.2.cloned.1.call-update) | async-done | bytes 262160 | tf_op jit(solution)/shard_map/psum | solution.py:87
  566.4 94.6 %reduce-scatter.6.cloned.1.call-done = f32[4,24,1024]{2,1,0:T(8,128)} async-done(((f32[4,384,1024]{2,1,0:T(8,128)}), f32[4,24,1024]{2,1,0:T(8,128)}) %reduce-scatter.6.cloned.1.call-update) | async-done | bytes 393232 | tf_op jit(solution)/shard_map/reduce_scatter | solution.py:126
  (86 shorter events, 30.3 us)
Async XLA Ops:
  8.0 141.9 %copy-start = (bf16[4,384,1024]{2,1,0:T(8,128)(2,1)S(1)}, bf16[4,384,1024]{2,1,0:T(8,128)(2,1)}, u32[]{:S(2)}) copy-start(bf16[4,384,1024]{2,1,0:T(8,128)(2,1)} %param.15) | copy-start | bytes 9437188
  8.0 45.8 %copy-start.1 = (bf16[128,1024]{1,0:T(8,128)(2,1)S(1)}, bf16[128,1024]{1,0:T(8,128)(2,1)}, u32[]{:S(2)}) copy-start(bf16[128,1024]{1,0:T(8,128)(2,1)} %param.9) | copy-start | bytes 786436
  61.8 81.5 %copy-start.4 = (bf16[4,384,1024]{2,1,0:T(8,128)(2,1)S(1)}, bf16[4,384,1024]{2,1,0:T(8,128)(2,1)}, u32[]{:S(2)}) copy-start(bf16[4,384,1024]{2,1,0:T(8,128)(2,1)} %param.13) | copy-start | bytes 9437188
  143.4 1.9 copy-start.2
  143.4 3.0 copy-start.6
  146.4 3.5 copy-start.12
  149.9 1.8 copy-start.7
  153.9 4.8 copy-start.11
  153.9 76.9 %all-to-all-start.1 = ((bf16[16,96,1024]{2,1,0:T(8,128)(2,1)}), bf16[16,96,1024]{2,1,0:T(8,128)(2,1)}, u32[]{:S(2)}, u32[]{:S(2)}) async-start(bf16[16,96,1024]{2,1,0:T(8,128)(2,1)} %bitcast.140), calls=%async_computation.1 | async-start | bytes 6291456 | tf_op jit(solution)/shard_map/all_to_all | solution.py:64
  257.8 78.0 %all-to-all-start.2 = ((bf16[16,96,1024]{2,1,0:T(8,128)(2,1)}), bf16[16,96,1024]{2,1,0:T(8,128)(2,1)}, u32[]{:S(2)}, u32[]{:S(2)}) async-start(bf16[16,96,1024]{2,1,0:T(8,128)(2,1)} %select_select_fusion), calls=%async_computation.2 | async-start | bytes 6291456 | tf_op jit(solution)/shard_map/all_to_all | solution.py:96
  265.2 301.2 %all-reduce.2.cloned.1.call-start = ((), (), s32[]{:S(2)}) async-start(), calls=%async_computation.7 | async-start | bytes 524288 | tf_op jit(solution)/shard_map/psum | solution.py:87
  266.3 300.1 %reduce-scatter.8.cloned.1.call-start = ((), (), s32[]{:S(2)}) async-start(), calls=%async_computation.10 | async-start | bytes 6684672 | tf_op jit(solution)/shard_map/reduce_scatter | solution.py:127
  342.6 223.9 %reduce-scatter.4.cloned.1.call-start = ((), (), s32[]{:S(2)}) async-start(), calls=%async_computation.8 | async-start | bytes 6684672 | tf_op jit(solution)/shard_map/reduce_scatter | solution.py:125
  342.6 7.9 %copy-start.3 = (bf16[16,96,1024]{2,1,0:T(8,128)(2,1)S(1)}, bf16[16,96,1024]{2,1,0:T(8,128)(2,1)}, u32[]{:S(2)}) copy-start(bf16[16,96,1024]{2,1,0:T(8,128)(2,1)} %copy-done.2) | copy-start | bytes 9437188
  349.5 1.1 copy-start.8
  355.1 306.0 %reduce-scatter.6.cloned.1.call-start = ((), (), s32[]{:S(2)}) async-start(), calls=%async_computation.9 | async-start | bytes 6684672 | tf_op jit(solution)/shard_map/reduce_scatter | solution.py:126
  362.2 4.6 copy-start.5
  362.2 4.6 copy-start.9
  458.3 5.2 copy-start.10
Sparse Core Ops, SparseCore 0:
  272.1 294.2 all-reduce.1
Sparse Core Ops, SparseCore 1:
  342.7 116.4 reduce-scatter.7
  464.0 96.0 reduce-scatter.3
  565.0 96.1 reduce-scatter.5
where the time goes:
time: 673 us; the launch traced here: 670 us
  waiting for transfers between devices  327 us (49%)
  blocking collectives  163 us (24%)
  local copies, waits for them, and re-layouts  55.1 us (8%)
  other arithmetic  54.9 us (8%)
  matrix products  41.6 us (6%)
  between operations  16 us (2%)
  starting transfers between devices  12.7 us (2%)
    psum x1, waiting for transfers between devices, body(): router_grad = lax.psum(router_part, ('dp', 'expert'))  102 us
    reduce_scatter x1, waiting for transfers between devices, body(): up_grad = lax.psum_scatter(full_up, 'dp', scatter_dimension=1, tiled=True)  94.6 us
    all_to_all x1, blocking collectives, body(): lax.all_to_all(send_rows, 'expert', split_axis=0, concat_axis=0, tiled=True)  81.5 us
    all_to_all x1, blocking collectives, body(): lax.all_to_all(row_grad.reshape(expert_peers, exp_dev * capacity, model_w...  81.1 us
    all_to_all x1, waiting for transfers between devices, body(): lax.all_to_all(send_grad, 'expert', split_axis=0, concat_axis=0, tiled=True)  69.4 us
    all_to_all x1, waiting for transfers between devices, body(): lax.all_to_all(produced.reshape(expert_peers, exp_dev * capacity, model_w...  61.6 us
    another operation x2, other arithmetic  34.2 us
    gather x2, local copies, waits for them, and re-layouts, fill_slots(): picked = jnp.take(source_rows, jnp.maximum(sources, 0) // divisor, axis=0)  15.5 us
  transfers between devices with their start and end apart: 6, of which 4 were waited for; matrix products, arithmetic and copies ran while one was open for 9% of the time, Pallas kernels for 0%

commit v1 on v0

--- a/solution.py
+++ b/solution.py
@@ -84,7 +84,7 @@
         jnp.where(expert_ids[:, :, None] == expert_cols, chosen_grad[:, :, None], 0.0), axis=1
     )
     router_part = jnp.dot(tokens.astype(jnp.float32).T, logit_grad, precision=lax.Precision.HIGHEST)
-    router_grad = lax.psum(router_part, ("dp", "expert"))
+    router_grad = jnp.sum(lax.all_gather(router_part, ("dp", "expert")), axis=0)
     router_input = jnp.dot(
         logit_grad, router_weight.astype(jnp.float32).T, precision=lax.Precision.HIGHEST
     )

time: 673 us -> 1250 us (1.86)
  the two profiles are of different devices: /device:TPU:2 before, /device:TPU:99 now
where the time goes in v1:
time: 1250 us
  waiting for transfers between devices  744 us (60%)
  blocking collectives  259 us (21%)
  local copies, waits for them, and re-layouts  109 us (9%)
  other arithmetic  75.2 us (6%)
  matrix products  42.4 us (3%)
  between operations  15.9 us (1%)
    all_gather x1, waiting for transfers between devices, body(): router_grad = jnp.sum(lax.all_gather(router_part, ('dp', 'expert')), axis=0)  683 us
    all_to_all x1, blocking collectives, body(): lax.all_to_all(send_grad, 'expert', split_axis=0, concat_axis=0, tiled=True)  92.9 us
    all_to_all x1, blocking collectives, body(): lax.all_to_all(row_grad.reshape(expert_peers, exp_dev * capacity, model_w...  87.9 us
    all_to_all x1, blocking collectives, body(): lax.all_to_all(send_rows, 'expert', split_axis=0, concat_axis=0, tiled=True)  78.2 us
    unnamed x38, local copies, waits for them, and re-layouts  61.5 us
    all_to_all x1, waiting for transfers between devices, body(): lax.all_to_all(produced.reshape(expert_peers, exp_dev * capacity, model_w...  60.5 us
    another operation x2, other arithmetic  34.2 us
  transfers between devices with their start and end apart: 5, of which 2 were waited for; matrix products, arithmetic and copies ran while one was open for 12% of the time, Pallas kernels for 0%

profile of v1, /device:TPU:99, one launch (start us, length us, event | category | flops | bytes accessed | tf_op | source)
XLA Modules:
  0.0 1251.5 jit_solution(9821530464806672302)
XLA Ops:
  10.9 34.2 %reduce-window.6 = s32[64,8,128]{2,1,0:T(8,128)} reduce-window(s32[64,8,128]{2,1,0:T(8,128)} %fusion.43, s32[]{:T(128)} %constant.85.clone.1), window={size=1x1x128 pad=0_0x0_0x127_0}, to_apply=%region_1.2 | reduce-window | flops 8323072 | bytes 524292 | tf_op jit(solution)/shard_map/reduce-window
  49.3 4.3 scatter_custom_fusion
  53.8 5.8 gather_fusion
  61.9 78.2 %all_to_all.20 = bf16[16,96,1024]{2,1,0:T(8,128)(2,1)S(1)} all-to-all(bf16[16,96,1024]{2,1,0:T(8,128)(2,1)S(1)} %select_select_fusion.1), channel_id=1, replica_groups=mesh['dp'=16,'expert'=16] {'expert'}, dimensions={0} | all-to-all | bytes 6291456 | tf_op jit(solution)/shard_map/all_to_all | solution.py:51
  143.0 3.5 fusion.27
  150.5 6.1 all-to-all-start.1
  159.9 7.0 gather_fusion.2
  167.2 60.5 %all-to-all-done.1 = bf16[16,96,1024]{2,1,0:T(8,128)(2,1)} async-done(((bf16[16,96,1024]{2,1,0:T(8,128)(2,1)}), bf16[16,96,1024]{2,1,0:T(8,128)(2,1)}, u32[]{:S(2)}, u32[]{:S(2)}) %all-to-all-start.1) | async-done | bytes 3145760 | tf_op jit(solution)/shard_map/all_to_all | solution.py:64
  227.6 8.3 gather_fusion.3
  240.1 2.6 fusion.2
  242.7 9.6 gather_fusion.1
  254.6 92.9 %all_to_all.21 = bf16[16,96,1024]{2,1,0:T(8,128)(2,1)S(1)} all-to-all(bf16[16,96,1024]{2,1,0:T(8,128)(2,1)S(1)} %select_select_fusion), channel_id=1, replica_groups=mesh['dp'=16,'expert'=16] {'expert'}, dimensions={0} | all-to-all | bytes 6291456 | tf_op jit(solution)/shard_map/all_to_all | solution.py:96
  347.5 3.3 fusion.25
  351.9 4.5 convolution_bitcast_fusion.1
  358.3 5.8 convolution_bitcast_fusion
  364.4 7.1 fusion.5
  371.4 4.5 fusion.20
  376.0 6.9 fusion.4
  383.3 87.9 %all_to_all.22 = bf16[16,96,1024]{2,1,0:T(8,128)(2,1)S(1)} all-to-all(bf16[16,96,1024]{2,1,0:T(8,128)(2,1)S(1)} %bitcast.145), channel_id=1, replica_groups=mesh['dp'=16,'expert'=16] {'expert'}, dimensions={0} | all-to-all | bytes 6291456 | tf_op jit(solution)/shard_map/all_to_all | solution.py:106
  471.2 5.4 gather_fusion.4
  476.6 5.2 convert_reduce_fusion
  482.9 683.1 %all-gather.3.cloned.1.call-done = f32[262144,64]{0,1:T(8,128)} async-done(((f32[1024,64]{0,1:T(8,128)}), f32[262144,64]{0,1:T(8,128)}) %all-gather.3.cloned.1.call-update) | async-done | bytes 67108880 | tf_op jit(solution)/shard_map/all_gather | solution.py:87
  1166.0 56.4 %copy.80 = f32[8,8,256,1024]{3,2,1,0:T(8,128)} copy(f32[8,8,256,1024]{3,1,2,0:T(8,128)} %bitcast.42) | data formatting | bytes 134217728
  1222.4 21.5 %bitcast_reduce_fusion = f32[1024,64]{0,1:T(8,128)} fusion(f32[8,8,256,1024]{3,2,1,0:T(8,128)} %copy.80), kind=kLoop, calls=%fused_computation.6 | loop fusion | flops 16711680 | bytes 67371008 | tf_op jit(solution)/shard_map/reduce_sum | solution.py:87
  (96 shorter events, 31.0 us)
Async XLA Ops:
  8.0 138.5 %copy-start = (bf16[4,384,1024]{2,1,0:T(8,128)(2,1)S(1)}, bf16[4,384,1024]{2,1,0:T(8,128)(2,1)}, u32[]{:S(2)}) copy-start(bf16[4,384,1024]{2,1,0:T(8,128)(2,1)} %param.15) | copy-start | bytes 9437188
  8.0 45.8 %copy-start.2 = (bf16[128,1024]{1,0:T(8,128)(2,1)S(1)}, bf16[128,1024]{1,0:T(8,128)(2,1)}, u32[]{:S(2)}) copy-start(bf16[128,1024]{1,0:T(8,128)(2,1)} %param.9) | copy-start | bytes 786436
  61.8 78.2 %copy-start.8 = (bf16[4,384,1024]{2,1,0:T(8,128)(2,1)S(1)}, bf16[4,384,1024]{2,1,0:T(8,128)(2,1)}, u32[]{:S(2)}) copy-start(bf16[4,384,1024]{2,1,0:T(8,128)(2,1)} %param.13) | copy-start | bytes 9437188
  140.0 1.9 copy-start.3
  140.0 3.0 copy-start.9
  143.0 3.5 copy-start.15
  146.5 1.8 copy-start.10
  150.5 8.1 copy-start.14
  150.5 77.1 %all-to-all-start.1 = ((bf16[16,96,1024]{2,1,0:T(8,128)(2,1)}), bf16[16,96,1024]{2,1,0:T(8,128)(2,1)}, u32[]{:S(2)}, u32[]{:S(2)}) async-start(bf16[16,96,1024]{2,1,0:T(8,128)(2,1)} %bitcast.144), calls=%async_computation.1 | async-start | bytes 6291456 | tf_op jit(solution)/shard_map/all_to_all | solution.py:64
  156.6 1009.4 %all-gather.3.cloned.1.call-start = ((), (), s32[]{:S(2)}) async-start(), calls=%async_computation.10 | async-start | bytes 67371008 | tf_op jit(solution)/shard_map/all_gather | solution.py:87
  239.7 1004.2 %reduce-scatter.4.cloned.1.call-start = ((), (), s32[]{:S(2)}) async-start(), calls=%async_computation.7 | async-start | bytes 6684672 | tf_op jit(solution)/shard_map/reduce_scatter | solution.py:125
  254.6 92.9 %copy-start.16 = (f32[4,16,24,384]{3,2,1,0:T(8,128)S(1)}, f32[4,16,24,384]{3,2,1,0:T(8,128)}, u32[]{:S(2)}) copy-start(f32[4,16,24,384]{3,2,1,0:T(8,128)} %copy-done.15) | copy-start | bytes 7077892
  254.6 92.9 %copy-start.17 = (f32[4,16,24,384]{3,2,1,0:T(8,128)S(1)}, f32[4,16,24,384]{3,2,1,0:T(8,128)}, u32[]{:S(2)}) copy-start(f32[4,16,24,384]{3,2,1,0:T(8,128)} %get-tuple-element.18) | copy-start | bytes 7077892
  347.5 3.3 copy-start.6
  347.5 4.4 copy-start.4
  350.8 1.0 copy-start.12
  356.4 1.9 copy-start.5
  356.4 887.5 %reduce-scatter.6.cloned.1.call-start = ((), (), s32[]{:S(2)}) async-start(), calls=%async_computation.8 | async-start | bytes 6684672 | tf_op jit(solution)/shard_map/reduce_scatter | solution.py:126
  364.1 7.4 copy-start.7
  364.1 879.9 %reduce-scatter.8.cloned.1.call-start = ((), (), s32[]{:S(2)}) async-start(), calls=%async_computation.9 | async-start | bytes 6684672 | tf_op jit(solution)/shard_map/reduce_scatter | solution.py:127
  364.3 7.1 copy-start.11
  476.5 5.2 copy-start.13
  1222.4 21.5 %copy-start.1 = (bf16[4,384,1024]{2,1,0:T(8,128)(2,1)S(1)}, bf16[4,384,1024]{2,1,0:T(8,128)(2,1)}, u32[]{:S(2)}) copy-start(bf16[4,384,1024]{2,1,0:T(8,128)(2,1)} %param.15) | copy-start | bytes 9437188
Sparse Core Ops, SparseCore 0:
  239.9 926.0 all-gather.2
Sparse Core Ops, SparseCore 1:
  356.5 110.5 reduce-scatter.3
  471.9 98.9 reduce-scatter.5
  575.7 97.3 reduce-scatter.7
